TPU v7x, 32 devices: a whole 2x2x4 slice. The times are simulated.
32 devices in a mesh: groups: 2 (over y), layer: 8 (over z, x), feat: 2 (over core).
Axes of the slice: x: 2, y: 2, z: 4, core: 2. Of those that a mesh axis runs over, the one named last changes fastest.
Arguments:
- codes_idx: int32 [64, 1, 64], P(('groups', 'layer', 'feat')), parts along dimension 0, may hold values from 0 to 16383, as said below
- codes_val: bfloat16 [64, 1, 64], P(('groups', 'layer', 'feat')), parts along dimension 0, may hold values from 0.19921875 to 4
- decoder: bfloat16 [16384, 2304], P(('layer', 'feat')), may hold values from -0.75 to 0.75
- bias: float32 [2304], replicated, may hold values from -3 to 3
- target: bfloat16 [64, 2304], P(('groups', 'layer', 'feat')), parts along dimension 0, may hold values from -6 to 6
Outputs:
- recon: float32 [64, 2304], P(('groups', 'layer', 'feat')), parts along dimension 0
- grad_decoder: bfloat16 [32768, 2304], P(('groups', 'layer', 'feat')), parts along dimension 0
- gradient_active_codes: float32 [64, 1, 64], P(('groups', 'layer', 'feat')), parts along dimension 0
There are 2 independent parts, one for each index of `groups`. A program takes and returns all parts, laid end to end along the dimension named above; an argument that names none is the same for every part. Nothing has to cross between parts.
Inputs may be any that keep to these rules, and one draw needn't show every extreme that they name: `codes_idx`: for each token and source layer, 64 different features of that layer's 16384, at most 16 of them in any aligned block of 1024 features, and exactly 16 in at least one such block; some 128-feature blocks are chosen far more often than others.
All inputs are finite; a program needn't handle non-finite values.
Results may differ from a plain program's by a relative error of at most 0.0048.
Values may be sent and summed in bfloat16 or wider, within the bound.
A program may use at most 64 MiB of HBM per device.

v0:
```python
import jax
import jax.numpy as jnp
from jax import lax
from jax.sharding import PartitionSpec as P

FEATURE_WIDTH = 16384


def per_device(codes_idx, codes_val, decoder, bias, target):
    tokens = codes_idx.shape[0]
    sources = codes_idx.shape[1]
    active = codes_idx.shape[2]
    rows = decoder.shape[0]
    devices = lax.axis_size(("layer", "feat"))
    total = rows * devices
    offsets = jnp.arange(sources, dtype=jnp.int32)[None, :, None] * FEATURE_WIDTH
    columns = (offsets + codes_idx).reshape(tokens, sources * active)
    line = jnp.arange(tokens, dtype=jnp.int32)[:, None]
    dense = (
        jnp.zeros((tokens, total), jnp.bfloat16)
        .at[line, columns]
        .set(codes_val.reshape(tokens, sources * active))
    )
    acts = lax.all_to_all(dense, ("layer", "feat"), split_axis=1, concat_axis=0, tiled=True)
    partial_value = jnp.dot(acts, decoder, preferred_element_type=jnp.float32)
    summed = lax.psum(partial_value, ("layer", "feat"))
    every_target_layer = lax.all_gather(target, ("layer", "feat"), axis=0, tiled=True)
    recon_all = summed + bias
    error = (recon_all - every_target_layer.astype(jnp.float32)).astype(jnp.bfloat16)
    grad_w = lax.dot_general(
        acts, error, (((0,), (0,)), ((), ())), preferred_element_type=jnp.float32
    )
    grad_dense = lax.dot_general(
        error, decoder, (((1,), (1,)), ((), ())), preferred_element_type=jnp.float32
    )
    first_row = lax.axis_index(("layer", "feat")) * tokens
    recon = lax.dynamic_slice_in_dim(recon_all, first_row, tokens, 0)
    returned = lax.all_to_all(
        grad_dense, ("layer", "feat"), split_axis=0, concat_axis=1, tiled=True
    )
    gradient_active_codes = jnp.take_along_axis(returned, columns, axis=1).reshape(
        tokens, sources, active
    )
    return (recon, grad_w.astype(jnp.bfloat16), gradient_active_codes)


def solution(mesh):
    placed = (
        P(("groups", "layer", "feat"), None, None),
        P(("groups", "layer", "feat"), None, None),
        P(("layer", "feat"), None),
        P(),
        P(("groups", "layer", "feat"), None),
    )
    return jax.shard_map(
        per_device,
        mesh=mesh,
        in_specs=placed,
        out_specs=(
            P(("groups", "layer", "feat"), None),
            P(("groups", "layer", "feat"), None),
            P(("groups", "layer", "feat"), None, None),
        ),
        check_vma=False,
    )
```

profile of v0, /device:TPU:0, one launch (start us, length us, event | category | flops | bytes accessed | tf_op | source)
XLA Modules:
  0.0 151.1 jit_solution(7768881133970282444)
XLA Ops:
  7.2 0.0 copy-start.1
  7.2 0.0 copy-start
  7.2 0.0 all-reduce.2.cloned.1.call-start
  7.2 0.7 reshape.69
  8.0 0.7 fusion.1
  8.7 0.1 reshape.67
  8.8 6.7 %scatter_fusion = bf16[2,16384]{1,0:T(2,128)(2,1)S(1)} fusion(bf16[2,16384]{1,0:T(2,128)(2,1)S(1)} %broadcast_in_dim.7, s32[128]{0:T(128)S(1)} %reshape.67, bf16[128]{0:T(256)(128)(2,1)S(1)} %reshape.69), kind=kCustom, calls=%fused_computation.1 | custom fusion | bytes 1792 | tf_op jit(solution)/shard_map/scatter | solution.py:22
  15.5 14.0 %all_to_all.38 = bf16[2,16,1024]{2,0,1:T(2,128)(2,1)S(1)} all-to-all(bf16[2,16,1024]{2,0,1:T(2,128)(2,1)S(1)} %bitcast.25), channel_id=1, replica_groups=mesh['groups'=2,'layer'=8,'feat'=2] {'layer','feat'}, dimensions={1} | all-to-all | bytes 131072 | tf_op jit(solution)/shard_map/all_to_all | solution.py:24
  29.6 4.0 %fusion.2 = f32[32,2304]{1,0:T(8,128)} fusion(bf16[32,1024]{1,0:T(8,128)(2,1)S(1)} %all_to_all.31, bf16[1024,2304]{1,0:T(8,128)(2,1)} %param.7), kind=kOutput, calls=%fused_computation.14 | convolution fusion | flops 150994944 | bytes 5079040 | tf_op jit(solution)/shard_map/dot_general | solution.py:25
  33.5 0.0 all-reduce.2.cloned.1.call-update
  33.6 0.1 reshape.61
  33.7 0.0 copy-done.1
  33.7 18.2 %all-gather = bf16[16,2,2304]{2,1,0:T(2,128)(2,1)S(1)} all-gather(bf16[1,2,2304]{2,1,0:T(2,128)(2,1)S(1)} %bitcast.27), channel_id=1, replica_groups=mesh['groups'=2,'layer'=8,'feat'=2] {'layer','feat'}, dimensions={0}, use_global_device_ids=true | all-gather | bytes 156672 | tf_op jit(solution)/shard_map/all_gather | solution.py:27
  51.9 69.4 %all-reduce.2.cloned.1.call-done = f32[32,2304]{1,0:T(8,128)} async-done(((f32[32,2304]{1,0:T(8,128)}), f32[32,2304]{1,0:T(8,128)}) %all-reduce.2.cloned.1.call-update) | async-done | bytes 294928 | tf_op jit(solution)/shard_map/psum | solution.py:26
  121.3 0.0 copy-done
  121.3 1.0 subtract_convert_fusion
  122.3 0.0 copy-start.2
  122.3 3.8 %fusion.3 = f32[32,1024]{1,0:T(8,128)S(1)} fusion(bf16[32,2304]{1,0:T(8,128)(2,1)S(1)} %get-tuple-element.12, bf16[1024,2304]{1,0:T(8,128)(2,1)} %param.7), kind=kOutput, calls=%fused_computation.15 | convolution fusion | flops 150994944 | bytes 4997120 | tf_op jit(solution)/shard_map/dot_general | solution.py:33
  126.1 3.6 %convolution_convert_fusion = bf16[1024,2304]{1,0:T(8,128)(2,1)} fusion(bf16[32,1024]{1,0:T(8,128)(2,1)S(1)} %all_to_all.31, bf16[32,2304]{1,0:T(8,128)(2,1)S(1)} %get-tuple-element.12), kind=kOutput, calls=%fused_computation.2 | convolution fusion | flops 153354240 | bytes 4931584 | tf_op jit(solution)/shard_map/dot_general | solution.py:30
  129.7 0.7 all_to_all.32
  130.4 3.7 %all-to-all-start.1 = ((f32[16,2,1024]{2,1,0:T(2,128)}), f32[16,2,1024]{2,1,0:T(2,128)S(1)}, u32[]{:S(2)}, u32[]{:S(2)}) async-start(f32[16,2,1024]{2,1,0:T(2,128)} %all_to_all.32), calls=%async_computation.1 | async-start | bytes 262144 | tf_op jit(solution)/shard_map/all_to_all | solution.py:38
  134.1 0.6 constant_dynamic-slice_fusion
  134.7 7.3 %all-to-all-done.1 = f32[16,2,1024]{2,1,0:T(2,128)S(1)} async-done(((f32[16,2,1024]{2,1,0:T(2,128)}), f32[16,2,1024]{2,1,0:T(2,128)S(1)}, u32[]{:S(2)}, u32[]{:S(2)}) %all-to-all-start.1) | async-done | bytes 131104 | tf_op jit(solution)/shard_map/all_to_all | solution.py:38
  142.1 1.5 %gather_fusion = f32[128]{0:T(128)S(1)} fusion(f32[2,16384]{1,0:T(2,128)S(1)} %bitcast.24, s32[128]{0:T(128)S(1)} %reshape.61), kind=kCustom, calls=%fused_computation | custom fusion | bytes 2048 | tf_op jit(solution)/shard_map/jit(take_along_axis)/gather | solution.py:41
  143.6 0.1 gather.7
  143.7 0.0 copy-done.2
  143.7 0.6 and_select_fusion
  (3 shorter events, 0.1 us)
Async XLA Ops:
  7.2 26.5 %copy-start.1 = (bf16[2,2304]{1,0:T(2,128)(2,1)S(1)}, bf16[2,2304]{1,0:T(2,128)(2,1)}, u32[]{:S(2)}) copy-start(bf16[2,2304]{1,0:T(2,128)(2,1)} %param.9) | copy-start | bytes 27652
  7.2 114.1 %copy-start = (f32[2304]{0:T(1024)S(1)}, f32[2304]{0:T(1024)}, u32[]{:S(2)}) copy-start(f32[2304]{0:T(1024)} %param.8) | copy-start | bytes 27652
  7.2 114.1 %all-reduce.2.cloned.1.call-start = ((), (), s32[]{:S(2)}) async-start(), calls=%async_computation.2 | async-start | bytes 589824 | tf_op jit(solution)/shard_map/psum | solution.py:26
  122.3 21.4 %copy-start.2 = (s32[2,1,64]{2,1,0:T(1,128)S(1)}, s32[2,1,64]{2,1,0:T(1,128)}, u32[]{:S(2)}) copy-start(s32[2,1,64]{2,1,0:T(1,128)} %param.5) | copy-start | bytes 1540
  130.4 11.6 %all-to-all-start.1 = ((f32[16,2,1024]{2,1,0:T(2,128)}), f32[16,2,1024]{2,1,0:T(2,128)S(1)}, u32[]{:S(2)}, u32[]{:S(2)}) async-start(f32[16,2,1024]{2,1,0:T(2,128)} %all_to_all.32), calls=%async_computation.1 | async-start | bytes 262144 | tf_op jit(solution)/shard_map/all_to_all | solution.py:38
Sparse Core Ops, SparseCore 0:
  33.7 87.5 all-reduce.1
where the time goes:
time: 152 us; the launch traced here: 151 us
  waiting for transfers between devices  76.7 us (50%)
  blocking collectives  32.2 us (21%)
  between operations  14.1 us (9%)
  matrix products  11.4 us (8%)
  local copies, waits for them, and re-layouts  10.7 us (7%)
  starting transfers between devices  3.73 us (2%)
  other arithmetic  2.26 us (1%)
    psum x1, waiting for transfers between devices, per_device(): summed = lax.psum(partial_value, ('layer', 'feat'))  69.4 us
    all_gather x1, blocking collectives, per_device(): lax.all_gather(target, ('layer', 'feat'), axis=0, tiled=True)  18.2 us
    all_to_all x1, blocking collectives, per_device(): lax.all_to_all(dense, ('layer', 'feat'), split_axis=1, concat_axis=0, til...  14 us
    all_to_all x1, waiting for transfers between devices, per_device(): lax.all_to_all(grad_dense, ('layer', 'feat'), split_axis=0, concat_axis=1...  7.31 us
    scatter x1, local copies, waits for them, and re-layouts, per_device(): dense = jnp.zeros((tokens, total), jnp.bfloat16).at[line, columns].set(co...  6.72 us
    dot_general x1, matrix products, per_device(): partial_value = jnp.dot(acts, decoder, preferred_element_type=jnp.float32)  3.97 us
    dot_general x1, matrix products, per_device(): lax.dot_general(error, decoder, (((1,), (1,)), ((), ())), preferred_eleme...  3.8 us
    all_to_all x1, starting transfers between devices, per_device(): lax.all_to_all(grad_dense, ('layer', 'feat'), split_axis=0, concat_axis=1...  3.69 us
  transfers between devices with their start and end apart: 2, of which 2 were waited for; matrix products, arithmetic and copies ran while one was open for 0% of the time, Pallas kernels for 0%

commit v1 on v0

v1 whole, which is shorter than its diff:
```python
import functools

import jax
import jax.numpy as jnp
from jax import lax
from jax.experimental import pallas as pl
from jax.experimental.pallas import tpu as pltpu
from jax.sharding import PartitionSpec as P

FEATURE_WIDTH = 16384
LANES = 128
MESH = pl.DeviceIdType.MESH
F32 = jnp.float32


def exchange_kernel(
    msg_ref, dec_hbm, bias_ref, target_ref,
    recon_ref, acts_ref, err_ref, grad_ref,
    dec, codes, wide, part, got, errs, gout, gin,
    dec_sem, send_sems, recv_sems,
):
    layers, feats = lax.axis_size("layer"), lax.axis_size("feat")
    n = layers * feats
    me = lax.axis_index("layer") * feats + lax.axis_index("feat")
    sources = msg_ref.shape[0]
    rows, width = dec.shape
    tokens = recon_ref.shape[0]
    blocks = rows // LANES
    span = n // sources
    base = lax.rem(me, span) * rows

    load = pltpu.make_async_copy(dec_hbm, dec, dec_sem)
    load.start()

    def place(t):
        return {"layer": t // feats, "feat": lax.rem(t, feats)}

    def others(body):
        def step(i, carry):
            body(lax.rem(me + i, n))
            return carry
        lax.fori_loop(1, n, step, 0)

    def send(src_of, dst, phase):
        def one(t):
            pltpu.make_async_remote_copy(
                src_ref=src_of(t), dst_ref=dst.at[me],
                send_sem=send_sems.at[phase], recv_sem=recv_sems.at[phase],
                device_id=place(t), device_id_type=MESH,
            ).start()
        others(one)

    def settle(buf, sem):
        view = buf.at[pl.ds(0, n - 1)]
        pltpu.make_async_copy(view, view, sem).wait()

    barrier = pltpu.get_barrier_semaphore()
    others(lambda t: pl.semaphore_signal(
        barrier, inc=1, device_id=place(t), device_id_type=MESH))
    pl.semaphore_wait(barrier, n - 1)

    send(lambda t: msg_ref.at[t // span], codes, 0)
    codes[me] = msg_ref[me // span]
    settle(codes, recv_sems.at[0])

    lane = lax.broadcasted_iota(jnp.int32, (1, LANES), 1)
    deep = lax.broadcasted_iota(jnp.int32, (LANES, LANES), 0)
    shelf = lax.broadcasted_iota(jnp.int32, (tokens * blocks, LANES), 0)
    k = LANES // tokens
    owner_ok = (shelf // blocks) == (lax.broadcasted_iota(jnp.int32, (tokens * blocks, LANES), 1) // k)
    block_of = lax.rem(shelf, blocks)

    def where_codes(d):
        pair = codes[d]
        local = pair[0:1].astype(jnp.int32) - base
        hi = jnp.right_shift(local, 7)
        lo = jnp.bitwise_and(local, LANES - 1)
        mine = owner_ok & (block_of == hi)
        onehot = jnp.where(deep == lo, 1.0, 0.0)
        return pair[1:2], mine, onehot

    def build(d, carry):
        val, mine, onehot = where_codes(d)
        a = jnp.where(mine, val, 0.0).astype(jnp.bfloat16)
        spread = lax.dot_general(
            a, onehot.astype(jnp.bfloat16), (((1,), (1,)), ((), ())), preferred_element_type=F32)
        wide[pl.ds(d * tokens, tokens)] = spread.reshape(tokens, blocks, LANES)
        return carry
    lax.fori_loop(0, n, build, 0, unroll=8)
    acts = jnp.concatenate(
        [wide[:, h, :].astype(jnp.bfloat16) for h in range(blocks)], axis=1)
    acts_ref[...] = acts

    load.wait()
    chunk = 768 if width % 768 == 0 else width
    for c in range(0, width, chunk):
        p = jnp.dot(acts, dec[:, c:c + chunk], preferred_element_type=F32)
        for d in range(n):
            part[d, :, c:c + chunk] = p[d * tokens:(d + 1) * tokens]
    send(lambda t: part.at[t], got, 1)
    got[me] = part[me]
    settle(got, recv_sems.at[1])

    total = got[0]
    for d in range(1, n):
        total += got[d]
    recon = total + bias_ref[...]
    recon_ref[...] = recon
    errs[me] = (recon - target_ref[...].astype(F32)).astype(jnp.bfloat16).astype(F32)
    send(lambda t: errs.at[me], errs, 2)
    settle(errs, recv_sems.at[2])

    err = jnp.concatenate([errs[d] for d in range(n)], axis=0).astype(jnp.bfloat16)
    err_ref[...] = err
    gd = lax.dot_general(err, dec[...], (((1,), (1,)), ((), ())), preferred_element_type=F32)
    for h in range(blocks):
        wide[:, h, :] = gd[:, h * LANES:(h + 1) * LANES]

    def pick(d, carry):
        _, mine, onehot = where_codes(d)
        g = wide[pl.ds(d * tokens, tokens)].reshape(tokens * blocks, LANES)
        taken = lax.dot_general(
            g, onehot, (((1,), (0,)), ((), ())), preferred_element_type=F32,
            precision=lax.Precision.HIGHEST)
        gout[d] = jnp.sum(jnp.where(mine, taken, 0.0), axis=0, keepdims=True)
        return carry
    lax.fori_loop(0, n, pick, 0, unroll=8)
    send(lambda t: gout.at[t], gin, 3)
    gin[me] = gout[me]
    settle(gin, recv_sems.at[3])
    for s in range(sources):
        grad_ref[s] = jnp.sum(gin[s * span:(s + 1) * span], axis=0)

    for phase, buf in ((0, codes), (1, got), (2, errs), (3, gin)):
        settle(buf, send_sems.at[phase])


def per_device(n, codes_idx, codes_val, decoder, bias, target):
    tokens, sources, active = codes_idx.shape
    rows, width = decoder.shape
    lanes = tokens * active
    msg = jnp.stack(
        [
            codes_idx.transpose(1, 0, 2).reshape(sources, lanes).astype(F32),
            codes_val.transpose(1, 0, 2).reshape(sources, lanes).astype(F32),
        ],
        axis=1,
    )
    everyone = n * tokens
    vmem = pl.BlockSpec(memory_space=pltpu.VMEM)
    recon, acts, err, grad = pl.pallas_call(
        exchange_kernel,
        out_shape=(
            jax.ShapeDtypeStruct((tokens, width), F32),
            jax.ShapeDtypeStruct((everyone, rows), jnp.bfloat16),
            jax.ShapeDtypeStruct((everyone, width), jnp.bfloat16),
            jax.ShapeDtypeStruct((sources, 1, lanes), F32),
        ),
        in_specs=[vmem, pl.BlockSpec(memory_space=pl.ANY), vmem, vmem],
        out_specs=(vmem, vmem, vmem, vmem),
        scratch_shapes=[
            pltpu.VMEM((rows, width), jnp.bfloat16),
            pltpu.VMEM((n, 2, lanes), F32),
            pltpu.VMEM((everyone, rows // LANES, LANES), F32),
            pltpu.VMEM((n, tokens, width), F32),
            pltpu.VMEM((n, tokens, width), F32),
            pltpu.VMEM((n, tokens, width), F32),
            pltpu.VMEM((n, 1, lanes), F32),
            pltpu.VMEM((n, 1, lanes), F32),
            pltpu.SemaphoreType.DMA,
            pltpu.SemaphoreType.DMA((4,)),
            pltpu.SemaphoreType.DMA((4,)),
        ],
        compiler_params=pltpu.CompilerParams(
            collective_id=0, has_side_effects=True, vmem_limit_bytes=40 * 1024 * 1024
        ),
    )(msg, decoder, bias.reshape(1, width), target)
    grad_w = lax.dot_general(
        acts, err, (((0,), (0,)), ((), ())), preferred_element_type=F32
    ).astype(jnp.bfloat16)
    gradient_active_codes = grad.reshape(sources, tokens, active).transpose(1, 0, 2)
    return recon, grad_w, gradient_active_codes


def solution(mesh):
    placed = (
        P(("groups", "layer", "feat"), None, None),
        P(("groups", "layer", "feat"), None, None),
        P(("layer", "feat"), None),
        P(),
        P(("groups", "layer", "feat"), None),
    )
    return jax.shard_map(
        functools.partial(per_device, mesh.shape["layer"] * mesh.shape["feat"]),
        mesh=mesh,
        in_specs=placed,
        out_specs=(
            P(("groups", "layer", "feat"), None),
            P(("groups", "layer", "feat"), None),
            P(("groups", "layer", "feat"), None, None),
        ),
        check_vma=False,
    )
```

time: 152 us -> 47.5 us (0.31)
  waiting for transfers between devices: 76.7 us -> 0 us
  Pallas kernels: 0 us -> 35.2 us
  blocking collectives: 32.2 us -> 0 us
  between operations: 14.1 us -> 0.64 us
  matrix products: 11.4 us -> 3.6 us
  local copies, waits for them, and re-layouts: 10.7 us -> 6.33 us
  starting transfers between devices: 3.73 us -> 0 us
    psum x1 -> x0, waiting for transfers between devices: 69.4 us -> none  [per_device(): summed = lax.psum(partial_value, ('layer', 'feat'))]
    pallas_call x0 -> x1, Pallas kernels: none -> 35.2 us  [per_device(): pl.pallas_call(exchange_kernel, out_shape=(jax.ShapeDtypeStruct((tokens,...]
    all_gather x1 -> x0, blocking collectives: 18.2 us -> none  [per_device(): lax.all_gather(target, ('layer', 'feat'), axis=0, tiled=True)]
    all_to_all x1 -> x0, blocking collectives: 14 us -> none  [per_device(): lax.all_to_all(dense, ('layer', 'feat'), split_axis=1, concat_axis=0, til...]
    dot_general x3 -> x1, matrix products: 11.4 us -> 3.6 us  [per_device(): lax.dot_general(acts, err, (((0,), (0,)), ((), ())), preferred_element_ty...]
    all_to_all x1 -> x0, waiting for transfers between devices: 7.31 us -> none  [per_device(): lax.all_to_all(grad_dense, ('layer', 'feat'), split_axis=0, concat_axis=1...]
    scatter x1 -> x0, local copies, waits for them, and re-layouts: 6.72 us -> none  [per_device(): dense = jnp.zeros((tokens, total), jnp.bfloat16).at[line, columns].set(co...]
    all_to_all x1 -> x0, starting transfers between devices: 3.69 us -> none  [per_device(): lax.all_to_all(grad_dense, ('layer', 'feat'), split_axis=0, concat_axis=1...]
  transfers between devices with their start and end apart: 2 -> 0, of which waited for: 2 -> 0; matrix products, arithmetic and copies ran while one was open for 0% -> 0% of each run, Pallas kernels for 0% -> 0%
where the time goes in v1:
time: 47.5 us; the launch traced here: 47.1 us
  Pallas kernels  35.2 us (74%)
  local copies, waits for them, and re-layouts  6.33 us (13%)
  matrix products  3.6 us (8%)
  other arithmetic  1.37 us (3%)
  between operations  0.64 us (1%)
    pallas_call x1, Pallas kernels, per_device(): pl.pallas_call(exchange_kernel, out_shape=(jax.ShapeDtypeStruct((tokens,...  35.2 us
    unnamed x5, local copies, waits for them, and re-layouts  3.64 us
    dot_general x1, matrix products, per_device(): lax.dot_general(acts, err, (((0,), (0,)), ((), ())), preferred_element_ty...  3.6 us

profile of v1, /device:TPU:0, one launch (start us, length us, event | category | flops | bytes accessed | tf_op | source)
XLA Modules:
  0.0 47.1 jit_solution(11912043701383226378)
XLA Ops:
  0.6 0.7 %reshape.38.bias_ref = f32[1,2304]{1,0:T(1,128)S(1)} reshape(f32[2304]{0:T(1024)} %param.8) | data formatting | bytes 18432 | tf_op jit(solution)/shard_map/reshape | solution.py:177
  1.3 0.7 %convert_reduce_fusion = f32[2,64]{1,0:T(2,128)S(1)} fusion(s32[2,1,64]{2,1,0:T(1,128)} %param.5), kind=kLoop, calls=%fused_computation.2 | loop fusion | flops 128 | bytes 1024 | tf_op jit(solution)/shard_map/convert_element_type | solution.py:144
  2.0 0.1 convert_element_type.34
  2.1 0.7 %reshape.39 = f32[1,1,128]{2,1,0:T(1,128)S(1)} reshape(bf16[2,1,64]{2,0,1:T(2,128)(2,1)} %param.6) | data formatting | bytes 768 | tf_op jit(solution)/shard_map/convert_element_type | solution.py:145
  2.9 0.0 copy-start
  2.9 2.3 %copy-done = bf16[1024,2304]{1,0:T(8,128)(2,1)S(1)} copy-done((bf16[1024,2304]{1,0:T(8,128)(2,1)S(1)}, bf16[1024,2304]{1,0:T(8,128)(2,1)}, u32[]{:S(2)}) %copy-start) | copy-done | bytes 4718616
  5.2 0.0 copy-start.1
  5.2 0.7 %copy-done.1 = bf16[2,2304]{1,0:T(2,128)(2,1)S(1)} copy-done((bf16[2,2304]{1,0:T(2,128)(2,1)S(1)}, bf16[2,2304]{1,0:T(2,128)(2,1)}, u32[]{:S(2)}) %copy-start.1) | copy-done | bytes 9240
  5.9 35.2 %shard_map.76 = (f32[2,2304]{1,0:T(2,128)S(1)}, bf16[32,1024]{1,0:T(8,128)(2,1)S(1)}, bf16[32,2304]{1,0:T(8,128)(2,1)S(1)}, f32[1,1,128]{2,1,0:T(1,128)S(1)}) custom-call(f32[1,2,128]{2,1,0:T(2,128)S(1)} %pad_maximum_fusion.msg_ref, bf16[1024,2304]{1,0:T(8,128)(2,1)S(1)} %copy-done, f32[1,2304]{1,0:T(1,128)S(1)} %reshape.38.bias_ref, ...), custom_call_target="tpu_custom_call" | custom-call | tf_op jit(solution)/shard_map/pallas_call | solution.py:151
  41.1 3.6 %convolution_convert_fusion = bf16[1024,2304]{1,0:T(8,128)(2,1)} fusion(bf16[32,1024]{1,0:T(8,128)(2,1)S(1)} %get-tuple-element.8, bf16[32,2304]{1,0:T(8,128)(2,1)S(1)} %get-tuple-element.9), kind=kOutput, calls=%fused_computation | convolution fusion | flops 153354240 | bytes 4931584 | tf_op jit(solution)/shard_map/dot_general | solution.py:178
  44.7 0.5 %broadcast.6 = f32[]{:T(128)} broadcast(f32[]{:T(128)} %constant.8), dimensions={} | broadcast | bytes 8 | tf_op jit(solution)/shard_map/pallas_call | solution.py:151
  45.2 0.7 %reduce.7 = f32[128]{0:T(128)S(1)} reduce(f32[1,1,128]{2,1,0:T(1,128)S(1)} %get-tuple-element.10, f32[]{:T(128)} %broadcast.6), dimensions={0,1}, to_apply=%get-tuple-element.10.reduce_sub_computation.3 | reduce | bytes 1028 | tf_op jit(solution)/shard_map/pallas_call | solution.py:151
  45.9 0.6 %transpose_reshape.3 = f32[2,1,64]{2,0,1:T(2,128)} reshape(f32[128]{0:T(128)S(1)} %reduce.7) | data formatting | bytes 1024 | tf_op jit(solution)/shard_map/transpose;reshape | solution.py:181
  46.5 0.6 %copy.10 = f32[2,2304]{1,0:T(2,128)} copy(f32[2,2304]{1,0:T(2,128)S(1)} %get-tuple-element.17) | data formatting | bytes 36864
  (1 shorter events, 0.0 us)
Async XLA Ops:
  2.9 2.3 %copy-start = (bf16[1024,2304]{1,0:T(8,128)(2,1)S(1)}, bf16[1024,2304]{1,0:T(8,128)(2,1)}, u32[]{:S(2)}) copy-start(bf16[1024,2304]{1,0:T(8,128)(2,1)} %dec_hbm.1) | copy-start | bytes 14155780
  5.2 0.7 %copy-start.1 = (bf16[2,2304]{1,0:T(2,128)(2,1)S(1)}, bf16[2,2304]{1,0:T(2,128)(2,1)}, u32[]{:S(2)}) copy-start(bf16[2,2304]{1,0:T(2,128)(2,1)} %target_ref.1) | copy-start | bytes 27652

commit v2 on v1

--- a/solution.py
+++ b/solution.py
@@ -14,23 +14,32 @@
 
 
 def exchange_kernel(
-    msg_ref, dec_hbm, bias_ref, target_ref,
+    idx_ref, val_ref, dec_hbm, bias_hbm, target_hbm,
     recon_ref, acts_ref, err_ref, grad_ref,
-    dec, codes, wide, part, got, errs, gout, gin,
-    dec_sem, send_sems, recv_sems,
+    dec, bias, target, msg, codes, wide, part, got, errs, gout, gin,
+    load_sems, send_sems, recv_sems,
 ):
     layers, feats = lax.axis_size("layer"), lax.axis_size("feat")
     n = layers * feats
     me = lax.axis_index("layer") * feats + lax.axis_index("feat")
-    sources = msg_ref.shape[0]
+    sources = msg.shape[0]
     rows, width = dec.shape
     tokens = recon_ref.shape[0]
     blocks = rows // LANES
     span = n // sources
     base = lax.rem(me, span) * rows
 
-    load = pltpu.make_async_copy(dec_hbm, dec, dec_sem)
-    load.start()
+    loads = [
+        pltpu.make_async_copy(src, dst, load_sems.at[i])
+        for i, (src, dst) in enumerate(((dec_hbm, dec), (bias_hbm, bias), (target_hbm, target)))
+    ]
+    for load in loads:
+        load.start()
+    for s in range(sources):
+        idx = [idx_ref[t, s:s + 1, :].astype(F32) for t in range(tokens)]
+        val = val_ref[s].astype(F32)
+        msg[s, 0:1] = jnp.concatenate(idx, axis=1)
+        msg[s, 1:2] = jnp.concatenate([val[t:t + 1] for t in range(tokens)], axis=1)
 
     def place(t):
         return {"layer": t // feats, "feat": lax.rem(t, feats)}
@@ -59,8 +68,8 @@
         barrier, inc=1, device_id=place(t), device_id_type=MESH))
     pl.semaphore_wait(barrier, n - 1)
 
-    send(lambda t: msg_ref.at[t // span], codes, 0)
-    codes[me] = msg_ref[me // span]
+    send(lambda t: msg.at[t // span], codes, 0)
+    codes[me] = msg[me // span]
     settle(codes, recv_sems.at[0])
 
     lane = lax.broadcasted_iota(jnp.int32, (1, LANES), 1)
@@ -91,7 +100,7 @@
         [wide[:, h, :].astype(jnp.bfloat16) for h in range(blocks)], axis=1)
     acts_ref[...] = acts
 
-    load.wait()
+    loads[0].wait()
     chunk = 768 if width % 768 == 0 else width
     for c in range(0, width, chunk):
         p = jnp.dot(acts, dec[:, c:c + chunk], preferred_element_type=F32)
@@ -101,12 +110,14 @@
     got[me] = part[me]
     settle(got, recv_sems.at[1])
 
+    loads[1].wait()
+    loads[2].wait()
     total = got[0]
     for d in range(1, n):
         total += got[d]
-    recon = total + bias_ref[...]
+    recon = total + bias[...][None, :]
     recon_ref[...] = recon
-    errs[me] = (recon - target_ref[...].astype(F32)).astype(jnp.bfloat16).astype(F32)
+    errs[me] = (recon - target[...].astype(F32)).astype(jnp.bfloat16).astype(F32)
     send(lambda t: errs.at[me], errs, 2)
     settle(errs, recv_sems.at[2])
 
@@ -135,19 +146,46 @@
         settle(buf, send_sems.at[phase])
 
 
+def finish_kernel(
+    acts_ref, err_ref, recon_ref, grad_ref,
+    recon_hbm, gw_hbm, codes_hbm,
+    gw, codes, sems,
+):
+    rows = gw.shape[0]
+    sources, _, lanes = grad_ref.shape
+    tokens = codes.shape[0]
+    active = lanes // tokens
+    for s in range(sources):
+        line = grad_ref[s]
+        for t in range(tokens):
+            codes[t, s:s + 1, :] = line[:, t * active:(t + 1) * active]
+    copies = [
+        pltpu.make_async_copy(recon_ref, recon_hbm, sems.at[0]),
+        pltpu.make_async_copy(codes, codes_hbm, sems.at[1]),
+    ]
+    for copy in copies:
+        copy.start()
+    err = err_ref[...]
+    step = 256
+    for i, r in enumerate(range(0, rows, step)):
+        gw[r:r + step] = lax.dot_general(
+            acts_ref[:, r:r + step], err, (((0,), (0,)), ((), ())), preferred_element_type=F32
+        ).astype(jnp.bfloat16)
+        copy = pltpu.make_async_copy(
+            gw.at[pl.ds(r, step)], gw_hbm.at[pl.ds(r, step)], sems.at[2 + i])
+        copy.start()
+        copies.append(copy)
+    for copy in copies:
+        copy.wait()
+
+
 def per_device(n, codes_idx, codes_val, decoder, bias, target):
     tokens, sources, active = codes_idx.shape
     rows, width = decoder.shape
     lanes = tokens * active
-    msg = jnp.stack(
-        [
-            codes_idx.transpose(1, 0, 2).reshape(sources, lanes).astype(F32),
-            codes_val.transpose(1, 0, 2).reshape(sources, lanes).astype(F32),
-        ],
-        axis=1,
-    )
     everyone = n * tokens
     vmem = pl.BlockSpec(memory_space=pltpu.VMEM)
+    hbm = pl.BlockSpec(memory_space=pl.ANY)
     recon, acts, err, grad = pl.pallas_call(
         exchange_kernel,
         out_shape=(
@@ -156,10 +194,13 @@
             jax.ShapeDtypeStruct((everyone, width), jnp.bfloat16),
             jax.ShapeDtypeStruct((sources, 1, lanes), F32),
         ),
-        in_specs=[vmem, pl.BlockSpec(memory_space=pl.ANY), vmem, vmem],
+        in_specs=[vmem, vmem, hbm, hbm, hbm],
         out_specs=(vmem, vmem, vmem, vmem),
         scratch_shapes=[
             pltpu.VMEM((rows, width), jnp.bfloat16),
+            pltpu.VMEM((width,), F32),
+            pltpu.VMEM((tokens, width), jnp.bfloat16),
+            pltpu.VMEM((sources, 2, lanes), F32),
             pltpu.VMEM((n, 2, lanes), F32),
             pltpu.VMEM((everyone, rows // LANES, LANES), F32),
             pltpu.VMEM((n, tokens, width), F32),
@@ -167,19 +208,30 @@
             pltpu.VMEM((n, tokens, width), F32),
             pltpu.VMEM((n, 1, lanes), F32),
             pltpu.VMEM((n, 1, lanes), F32),
-            pltpu.SemaphoreType.DMA,
+            pltpu.SemaphoreType.DMA((3,)),
             pltpu.SemaphoreType.DMA((4,)),
             pltpu.SemaphoreType.DMA((4,)),
         ],
         compiler_params=pltpu.CompilerParams(
-            collective_id=0, has_side_effects=True, vmem_limit_bytes=40 * 1024 * 1024
-        ),
-    )(msg, decoder, bias.reshape(1, width), target)
-    grad_w = lax.dot_general(
-        acts, err, (((0,), (0,)), ((), ())), preferred_element_type=F32
-    ).astype(jnp.bfloat16)
-    gradient_active_codes = grad.reshape(sources, tokens, active).transpose(1, 0, 2)
-    return recon, grad_w, gradient_active_codes
+            collective_id=0, has_side_effects=True, vmem_limit_bytes=56 * 1024 * 1024
+        ),
+    )(codes_idx, codes_val.transpose(1, 0, 2), decoder, bias, target)
+    return pl.pallas_call(
+        finish_kernel,
+        out_shape=(
+            jax.ShapeDtypeStruct((tokens, width), F32),
+            jax.ShapeDtypeStruct((rows, width), jnp.bfloat16),
+            jax.ShapeDtypeStruct((tokens, sources, active), F32),
+        ),
+        in_specs=[vmem, vmem, vmem, vmem],
+        out_specs=(hbm, hbm, hbm),
+        scratch_shapes=[
+            pltpu.VMEM((rows, width), jnp.bfloat16),
+            pltpu.VMEM((tokens, sources, active), F32),
+            pltpu.SemaphoreType.DMA((2 + rows // 256,)),
+        ],
+        compiler_params=pltpu.CompilerParams(vmem_limit_bytes=56 * 1024 * 1024),
+    )(acts, err, recon, grad)
 
 
 def solution(mesh):

time: 47.5 us -> 40.7 us (0.86)
  local copies, waits for them, and re-layouts: 6.33 us -> 0 us
  Pallas kernels: 35.2 us -> 39.9 us
  matrix products: 3.6 us -> 0 us
  other arithmetic: 1.37 us -> 0 us
    pallas_call x0 -> x1, Pallas kernels: none -> 3.67 us  [per_device(): pl.pallas_call(finish_kernel, out_shape=(jax.ShapeDtypeStruct((tokens, wi...]
    unnamed x5 -> x0, local copies, waits for them, and re-layouts: 3.64 us -> none
    dot_general x1 -> x0, matrix products: 3.6 us -> none  [per_device(): lax.dot_general(acts, err, (((0,), (0,)), ((), ())), preferred_element_ty...]
    pallas_call x1, Pallas kernels: 35.2 us -> 36.2 us  [per_device(): pl.pallas_call(exchange_kernel, out_shape=(jax.ShapeDtypeStruct((tokens,...]
    convert_element_type x2 -> x0, local copies, waits for them, and re-layouts: 0.82 us -> none  [the longest x1 0.74 us: per_device(): codes_val.transpose(1, 0, 2).reshape(sources, lanes).astype(F32)]
    reshape x1 -> x0, local copies, waits for them, and re-layouts: 0.71 us -> none  [per_device(): bias.reshape(1, width)]
    convert_element_type x1 -> x0, other arithmetic: 0.7 us -> none  [per_device(): codes_idx.transpose(1, 0, 2).reshape(sources, lanes).astype(F32)]
    pallas_call x1 -> x0, other arithmetic: 0.66 us -> none  [per_device(): pl.pallas_call(exchange_kernel, out_shape=(jax.ShapeDtypeStruct((tokens,...]
where the time goes in v2:
time: 40.7 us; the launch traced here: 40.5 us
  Pallas kernels  39.9 us (98%)
  between operations  0.64 us (2%)
    pallas_call x1, Pallas kernels, per_device(): pl.pallas_call(exchange_kernel, out_shape=(jax.ShapeDtypeStruct((tokens,...  36.2 us
    pallas_call x1, Pallas kernels, per_device(): pl.pallas_call(finish_kernel, out_shape=(jax.ShapeDtypeStruct((tokens, wi...  3.67 us

profile of v2, /device:TPU:0, one launch (start us, length us, event | category | flops | bytes accessed | tf_op | source)
XLA Modules:
  0.0 40.5 jit_solution(13472472519160892353)
XLA Ops:
  0.6 36.2 %shard_map.76 = (f32[2,2304]{1,0:T(2,128)}, bf16[32,1024]{1,0:T(8,128)(2,1)}, bf16[32,2304]{1,0:T(8,128)(2,1)}, f32[1,1,128]{2,1,0:T(1,128)}) custom-call(s32[2,1,64]{2,1,0:T(1,128)} %idx_ref.1, bf16[1,2,64]{2,1,0:T(2,128)(2,1)} %bitcast.1, bf16[1024,2304]{1,0:T(8,128)(2,1)} %dec_hbm.1, f32[2304]{0:T(1024)} %bias_hbm.1, bf16[2,2304]{1,0:T(2,128)(2,1)} %target_hbm.1), custom_call_target="tpu_custom_call" | custom-call | tf_op jit(solution)/shard_map/pallas_call | solution.py:189
  36.9 3.7 %shard_map.77 = (f32[2,2304]{1,0:T(2,128)}, bf16[1024,2304]{1,0:T(8,128)(2,1)}, f32[2,1,64]{2,1,0:T(1,128)}) custom-call(bf16[32,1024]{1,0:T(8,128)(2,1)} %get-tuple-element.7.acts_ref, bf16[32,2304]{1,0:T(8,128)(2,1)} %get-tuple-element.8.err_ref, f32[2,2304]{1,0:T(2,128)} %get-tuple-element.9.recon_ref, f32[1,1,128]{2,1,0:T(1,128)} %get-tuple-element.10.grad_ref), custom_call_target="tpu_custom_call" | custom-call | tf_op jit(solution)/shard_map/pallas_call | solution.py:219

commit v3 on v2

--- a/solution.py
+++ b/solution.py
@@ -9,6 +9,7 @@
 
 FEATURE_WIDTH = 16384
 LANES = 128
+WIRE = jnp.bfloat16
 MESH = pl.DeviceIdType.MESH
 F32 = jnp.float32
 
@@ -16,18 +17,23 @@
 def exchange_kernel(
     idx_ref, val_ref, dec_hbm, bias_hbm, target_hbm,
     recon_ref, acts_ref, err_ref, grad_ref,
-    dec, bias, target, msg, codes, wide, part, got, errs, gout, gin,
+    dec, bias, target, msg, codes, wide, part, half, outgoing, incoming, errs, gout, gin,
     load_sems, send_sems, recv_sems,
 ):
     layers, feats = lax.axis_size("layer"), lax.axis_size("feat")
+    my_layer, my_feat = lax.axis_index("layer"), lax.axis_index("feat")
     n = layers * feats
-    me = lax.axis_index("layer") * feats + lax.axis_index("feat")
+    me = my_feat * layers + my_layer
+    partner = 1 - my_feat
     sources = msg.shape[0]
     rows, width = dec.shape
     tokens = recon_ref.shape[0]
     blocks = rows // LANES
     span = n // sources
-    base = lax.rem(me, span) * rows
+    device = my_layer * feats + my_feat
+    base = lax.rem(device, span) * rows
+    chunks, chunk = part.shape[0], part.shape[-1]
+    sent = []
 
     loads = [
         pltpu.make_async_copy(src, dst, load_sems.at[i])
@@ -42,7 +48,10 @@
         msg[s, 1:2] = jnp.concatenate([val[t:t + 1] for t in range(tokens)], axis=1)
 
     def place(t):
-        return {"layer": t // feats, "feat": lax.rem(t, feats)}
+        return {"layer": lax.rem(t, layers), "feat": t // layers}
+
+    def source_of(t):
+        return (lax.rem(t, layers) * feats + t // layers) // span
 
     def others(body):
         def step(i, carry):
@@ -50,33 +59,39 @@
             return carry
         lax.fori_loop(1, n, step, 0)
 
-    def send(src_of, dst, phase):
-        def one(t):
-            pltpu.make_async_remote_copy(
-                src_ref=src_of(t), dst_ref=dst.at[me],
-                send_sem=send_sems.at[phase], recv_sem=recv_sems.at[phase],
-                device_id=place(t), device_id_type=MESH,
-            ).start()
-        others(one)
-
-    def settle(buf, sem):
-        view = buf.at[pl.ds(0, n - 1)]
+    def other_layers(body):
+        def step(i, carry):
+            body(lax.rem(my_layer + i, layers))
+            return carry
+        lax.fori_loop(1, layers, step, 0)
+
+    def push(src, dst, phase, where):
+        pltpu.make_async_remote_copy(
+            src_ref=src, dst_ref=dst,
+            send_sem=send_sems.at[phase], recv_sem=recv_sems.at[phase],
+            device_id=where, device_id_type=MESH,
+        ).start()
+
+    def settle(view, sem):
         pltpu.make_async_copy(view, view, sem).wait()
+
+    def arrive(view, phase):
+        settle(view, recv_sems.at[phase])
+        sent.append((view, phase))
 
     barrier = pltpu.get_barrier_semaphore()
     others(lambda t: pl.semaphore_signal(
         barrier, inc=1, device_id=place(t), device_id_type=MESH))
     pl.semaphore_wait(barrier, n - 1)
 
-    send(lambda t: msg.at[t // span], codes, 0)
-    codes[me] = msg[me // span]
-    settle(codes, recv_sems.at[0])
-
-    lane = lax.broadcasted_iota(jnp.int32, (1, LANES), 1)
+    others(lambda t: push(msg.at[source_of(t)], codes.at[me], 0, place(t)))
+    codes[me] = msg[device // span]
+    arrive(codes.at[pl.ds(0, n - 1)], 0)
+
+    lane = lax.broadcasted_iota(jnp.int32, (tokens * blocks, LANES), 1)
     deep = lax.broadcasted_iota(jnp.int32, (LANES, LANES), 0)
     shelf = lax.broadcasted_iota(jnp.int32, (tokens * blocks, LANES), 0)
-    k = LANES // tokens
-    owner_ok = (shelf // blocks) == (lax.broadcasted_iota(jnp.int32, (tokens * blocks, LANES), 1) // k)
+    owner_ok = (shelf // blocks) == (lane // (LANES // tokens))
     block_of = lax.rem(shelf, blocks)
 
     def where_codes(d):
@@ -85,14 +100,14 @@
         hi = jnp.right_shift(local, 7)
         lo = jnp.bitwise_and(local, LANES - 1)
         mine = owner_ok & (block_of == hi)
-        onehot = jnp.where(deep == lo, 1.0, 0.0)
+        onehot = jnp.where(deep == lo, 1.0, 0.0).astype(jnp.bfloat16)
         return pair[1:2], mine, onehot
 
     def build(d, carry):
         val, mine, onehot = where_codes(d)
         a = jnp.where(mine, val, 0.0).astype(jnp.bfloat16)
         spread = lax.dot_general(
-            a, onehot.astype(jnp.bfloat16), (((1,), (1,)), ((), ())), preferred_element_type=F32)
+            a, onehot, (((1,), (1,)), ((), ())), preferred_element_type=F32)
         wide[pl.ds(d * tokens, tokens)] = spread.reshape(tokens, blocks, LANES)
         return carry
     lax.fori_loop(0, n, build, 0, unroll=8)
@@ -100,50 +115,74 @@
         [wide[:, h, :].astype(jnp.bfloat16) for h in range(blocks)], axis=1)
     acts_ref[...] = acts
 
+    chip, cross, share, forward, back = (1, 1 + chunks, 1 + 2 * chunks, 1 + 3 * chunks, 1 + 4 * chunks)
     loads[0].wait()
-    chunk = 768 if width % 768 == 0 else width
-    for c in range(0, width, chunk):
-        p = jnp.dot(acts, dec[:, c:c + chunk], preferred_element_type=F32)
+    for c in range(chunks):
+        p = jnp.dot(acts, dec[:, c * chunk:(c + 1) * chunk], preferred_element_type=F32)
         for d in range(n):
-            part[d, :, c:c + chunk] = p[d * tokens:(d + 1) * tokens]
-    send(lambda t: part.at[t], got, 1)
-    got[me] = part[me]
-    settle(got, recv_sems.at[1])
-
+            part[c, d // layers, d % layers] = p[d * tokens:(d + 1) * tokens]
+        push(part.at[c, partner], half.at[c], chip + c, {"feat": partner})
+    for c in range(chunks):
+        arrive(half.at[c], chip + c)
+        outgoing[c] = (part[c, my_feat] + half[c]).astype(WIRE)
+        other_layers(lambda l, c=c: push(
+            outgoing.at[c, l], incoming.at[c, my_layer], cross + c, {"layer": l}))
+        incoming[c, my_layer] = outgoing[c, my_layer]
     loads[1].wait()
     loads[2].wait()
-    total = got[0]
-    for d in range(1, n):
-        total += got[d]
-    recon = total + bias[...][None, :]
-    recon_ref[...] = recon
-    errs[me] = (recon - target[...].astype(F32)).astype(jnp.bfloat16).astype(F32)
-    send(lambda t: errs.at[me], errs, 2)
-    settle(errs, recv_sems.at[2])
-
-    err = jnp.concatenate([errs[d] for d in range(n)], axis=0).astype(jnp.bfloat16)
-    err_ref[...] = err
-    gd = lax.dot_general(err, dec[...], (((1,), (1,)), ((), ())), preferred_element_type=F32)
+    for c in range(chunks):
+        cols = slice(c * chunk, (c + 1) * chunk)
+        arrive(incoming.at[c, pl.ds(0, layers - 1)], cross + c)
+        total = incoming[c, 0].astype(F32)
+        for l in range(1, layers):
+            total += incoming[c, l].astype(F32)
+        recon = total + bias[cols][None, :]
+        recon_ref[:, cols] = recon
+        errs[c, my_feat, my_layer] = (recon - target[:, cols].astype(F32)).astype(jnp.bfloat16)
+        mine_at = errs.at[c, my_feat, my_layer]
+        other_layers(lambda l, c=c, ref=mine_at: push(ref, ref, share + c, {"layer": l}))
+    for c in range(chunks):
+        arrive(errs.at[c, my_feat, pl.ds(0, layers - 1)], share + c)
+        push(errs.at[c, my_feat], errs.at[c, my_feat], forward + c, {"feat": partner})
+    gd = jnp.zeros((n * tokens, rows), F32)
+    for c in range(chunks):
+        cols = slice(c * chunk, (c + 1) * chunk)
+        arrive(errs.at[c, partner], forward + c)
+        err = jnp.concatenate(
+            [errs[c, d // layers, d % layers].astype(F32) for d in range(n)], axis=0
+        ).astype(jnp.bfloat16)
+        err_ref[:, cols] = err
+        gd += lax.dot_general(
+            err, dec[:, cols], (((1,), (1,)), ((), ())), preferred_element_type=F32)
     for h in range(blocks):
         wide[:, h, :] = gd[:, h * LANES:(h + 1) * LANES]
 
     def pick(d, carry):
         _, mine, onehot = where_codes(d)
         g = wide[pl.ds(d * tokens, tokens)].reshape(tokens * blocks, LANES)
-        taken = lax.dot_general(
-            g, onehot, (((1,), (0,)), ((), ())), preferred_element_type=F32,
-            precision=lax.Precision.HIGHEST)
+        high = g.astype(jnp.bfloat16)
+        rest = g - high.astype(F32)
+        middle = rest.astype(jnp.bfloat16)
+        low = (rest - middle.astype(F32)).astype(jnp.bfloat16)
+        taken = jnp.dot(
+            jnp.concatenate([high, middle, low], axis=0), onehot, preferred_element_type=F32)
+        rest_of = tokens * blocks
+        taken = taken[:rest_of] + taken[rest_of:2 * rest_of] + taken[2 * rest_of:]
         gout[d] = jnp.sum(jnp.where(mine, taken, 0.0), axis=0, keepdims=True)
         return carry
     lax.fori_loop(0, n, pick, 0, unroll=8)
-    send(lambda t: gout.at[t], gin, 3)
+    others(lambda t: push(gout.at[t], gin.at[me], back, place(t)))
     gin[me] = gout[me]
-    settle(gin, recv_sems.at[3])
+    arrive(gin.at[pl.ds(0, n - 1)], back)
+    per = span // feats
     for s in range(sources):
-        grad_ref[s] = jnp.sum(gin[s * span:(s + 1) * span], axis=0)
-
-    for phase, buf in ((0, codes), (1, got), (2, errs), (3, gin)):
-        settle(buf, send_sems.at[phase])
+        line = gin[s * per:(s + 1) * per]
+        for f in range(1, feats):
+            line += gin[f * layers + s * per:f * layers + (s + 1) * per]
+        grad_ref[s] = jnp.sum(line, axis=0)
+
+    for view, phase in sent:
+        settle(view, send_sems.at[phase])
 
 
 def finish_kernel(
@@ -179,11 +218,14 @@
         copy.wait()
 
 
-def per_device(n, codes_idx, codes_val, decoder, bias, target):
+def per_device(layers, feats, codes_idx, codes_val, decoder, bias, target):
     tokens, sources, active = codes_idx.shape
     rows, width = decoder.shape
     lanes = tokens * active
+    n = layers * feats
     everyone = n * tokens
+    chunks = 3
+    chunk = width // chunks
     vmem = pl.BlockSpec(memory_space=pltpu.VMEM)
     hbm = pl.BlockSpec(memory_space=pl.ANY)
     recon, acts, err, grad = pl.pallas_call(
@@ -203,14 +245,16 @@
             pltpu.VMEM((sources, 2, lanes), F32),
             pltpu.VMEM((n, 2, lanes), F32),
             pltpu.VMEM((everyone, rows // LANES, LANES), F32),
-            pltpu.VMEM((n, tokens, width), F32),
-            pltpu.VMEM((n, tokens, width), F32),
-            pltpu.VMEM((n, tokens, width), F32),
+            pltpu.VMEM((chunks, feats, layers, tokens, chunk), F32),
+            pltpu.VMEM((chunks, layers, tokens, chunk), F32),
+            pltpu.VMEM((chunks, layers, tokens, chunk), WIRE),
+            pltpu.VMEM((chunks, layers, tokens, chunk), WIRE),
+            pltpu.VMEM((chunks, feats, layers, tokens, chunk), jnp.bfloat16),
             pltpu.VMEM((n, 1, lanes), F32),
             pltpu.VMEM((n, 1, lanes), F32),
             pltpu.SemaphoreType.DMA((3,)),
-            pltpu.SemaphoreType.DMA((4,)),
-            pltpu.SemaphoreType.DMA((4,)),
+            pltpu.SemaphoreType.DMA((2 + 4 * chunks,)),
+            pltpu.SemaphoreType.DMA((2 + 4 * chunks,)),
         ],
         compiler_params=pltpu.CompilerParams(
             collective_id=0, has_side_effects=True, vmem_limit_bytes=56 * 1024 * 1024
@@ -243,7 +287,7 @@
         P(("groups", "layer", "feat"), None),
     )
     return jax.shard_map(
-        functools.partial(per_device, mesh.shape["layer"] * mesh.shape["feat"]),
+        functools.partial(per_device, mesh.shape["layer"], mesh.shape["feat"]),
         mesh=mesh,
         in_specs=placed,
         out_specs=(

time: 40.7 us -> 33.4 us (0.82)
  Pallas kernels: 39.9 us -> 32.6 us
    pallas_call x1, Pallas kernels: 36.2 us -> 28.9 us  [per_device(): pl.pallas_call(exchange_kernel, out_shape=(jax.ShapeDtypeStruct((tokens,...]
where the time goes in v3:
time: 33.4 us; the launch traced here: 33.2 us
  Pallas kernels  32.6 us (98%)
  between operations  0.64 us (2%)
    pallas_call x1, Pallas kernels, per_device(): pl.pallas_call(exchange_kernel, out_shape=(jax.ShapeDtypeStruct((tokens,...  28.9 us
    pallas_call x1, Pallas kernels, per_device(): pl.pallas_call(finish_kernel, out_shape=(jax.ShapeDtypeStruct((tokens, wi...  3.67 us

profile of v3, /device:TPU:0, one launch (start us, length us, event | category | flops | bytes accessed | tf_op | source)
XLA Modules:
  0.0 33.2 jit_solution(17203431351835768973)
XLA Ops:
  0.6 28.9 %shard_map.76 = (f32[2,2304]{1,0:T(2,128)}, bf16[32,1024]{1,0:T(8,128)(2,1)}, bf16[32,2304]{1,0:T(8,128)(2,1)}, f32[1,1,128]{2,1,0:T(1,128)}) custom-call(s32[2,1,64]{2,1,0:T(1,128)} %idx_ref.1, bf16[1,2,64]{2,1,0:T(2,128)(2,1)} %bitcast.1, bf16[1024,2304]{1,0:T(8,128)(2,1)} %dec_hbm.1, f32[2304]{0:T(1024)} %bias_hbm.1, bf16[2,2304]{1,0:T(2,128)(2,1)} %target_hbm.1), custom_call_target="tpu_custom_call" | custom-call | tf_op jit(solution)/shard_map/pallas_call | solution.py:231
  29.5 3.7 %shard_map.77 = (f32[2,2304]{1,0:T(2,128)}, bf16[1024,2304]{1,0:T(8,128)(2,1)}, f32[2,1,64]{2,1,0:T(1,128)}) custom-call(bf16[32,1024]{1,0:T(8,128)(2,1)} %get-tuple-element.7.acts_ref, bf16[32,2304]{1,0:T(8,128)(2,1)} %get-tuple-element.8.err_ref, f32[2,2304]{1,0:T(2,128)} %get-tuple-element.9.recon_ref, f32[1,1,128]{2,1,0:T(1,128)} %get-tuple-element.10.grad_ref), custom_call_target="tpu_custom_call" | custom-call | tf_op jit(solution)/shard_map/pallas_call | solution.py:263

commit v4 on v3

--- a/solution.py
+++ b/solution.py
@@ -17,14 +17,13 @@
 def exchange_kernel(
     idx_ref, val_ref, dec_hbm, bias_hbm, target_hbm,
     recon_ref, acts_ref, err_ref, grad_ref,
-    dec, bias, target, msg, codes, wide, part, half, outgoing, incoming, errs, gout, gin,
+    dec, bias, target, msg, codes, wide, outgoing, incoming, errs, gout, gin,
     load_sems, send_sems, recv_sems,
 ):
     layers, feats = lax.axis_size("layer"), lax.axis_size("feat")
     my_layer, my_feat = lax.axis_index("layer"), lax.axis_index("feat")
     n = layers * feats
     me = my_feat * layers + my_layer
-    partner = 1 - my_feat
     sources = msg.shape[0]
     rows, width = dec.shape
     tokens = recon_ref.shape[0]
@@ -32,7 +31,7 @@
     span = n // sources
     device = my_layer * feats + my_feat
     base = lax.rem(device, span) * rows
-    chunks, chunk = part.shape[0], part.shape[-1]
+    chunks, chunk = errs.shape[0], errs.shape[-1]
     sent = []
 
     loads = [
@@ -59,12 +58,6 @@
             return carry
         lax.fori_loop(1, n, step, 0)
 
-    def other_layers(body):
-        def step(i, carry):
-            body(lax.rem(my_layer + i, layers))
-            return carry
-        lax.fori_loop(1, layers, step, 0)
-
     def push(src, dst, phase, where):
         pltpu.make_async_remote_copy(
             src_ref=src, dst_ref=dst,
@@ -115,41 +108,33 @@
         [wide[:, h, :].astype(jnp.bfloat16) for h in range(blocks)], axis=1)
     acts_ref[...] = acts
 
-    chip, cross, share, forward, back = (1, 1 + chunks, 1 + 2 * chunks, 1 + 3 * chunks, 1 + 4 * chunks)
+    cross, share, back = 1, 1 + chunks, 1 + 2 * chunks
     loads[0].wait()
     for c in range(chunks):
         p = jnp.dot(acts, dec[:, c * chunk:(c + 1) * chunk], preferred_element_type=F32)
         for d in range(n):
-            part[c, d // layers, d % layers] = p[d * tokens:(d + 1) * tokens]
-        push(part.at[c, partner], half.at[c], chip + c, {"feat": partner})
-    for c in range(chunks):
-        arrive(half.at[c], chip + c)
-        outgoing[c] = (part[c, my_feat] + half[c]).astype(WIRE)
-        other_layers(lambda l, c=c: push(
-            outgoing.at[c, l], incoming.at[c, my_layer], cross + c, {"layer": l}))
-        incoming[c, my_layer] = outgoing[c, my_layer]
+            outgoing[c, d] = p[d * tokens:(d + 1) * tokens].astype(WIRE)
+        others(lambda t, c=c: push(outgoing.at[c, t], incoming.at[c, me], cross + c, place(t)))
+        incoming[c, me] = outgoing[c, me]
     loads[1].wait()
     loads[2].wait()
     for c in range(chunks):
         cols = slice(c * chunk, (c + 1) * chunk)
-        arrive(incoming.at[c, pl.ds(0, layers - 1)], cross + c)
+        arrive(incoming.at[c, pl.ds(0, n - 1)], cross + c)
         total = incoming[c, 0].astype(F32)
-        for l in range(1, layers):
-            total += incoming[c, l].astype(F32)
+        for d in range(1, n):
+            total += incoming[c, d].astype(F32)
         recon = total + bias[cols][None, :]
         recon_ref[:, cols] = recon
-        errs[c, my_feat, my_layer] = (recon - target[:, cols].astype(F32)).astype(jnp.bfloat16)
-        mine_at = errs.at[c, my_feat, my_layer]
-        other_layers(lambda l, c=c, ref=mine_at: push(ref, ref, share + c, {"layer": l}))
-    for c in range(chunks):
-        arrive(errs.at[c, my_feat, pl.ds(0, layers - 1)], share + c)
-        push(errs.at[c, my_feat], errs.at[c, my_feat], forward + c, {"feat": partner})
+        errs[c, me] = (recon - target[:, cols].astype(F32)).astype(jnp.bfloat16)
+        mine_at = errs.at[c, me]
+        others(lambda t, c=c, ref=mine_at: push(ref, ref, share + c, place(t)))
     gd = jnp.zeros((n * tokens, rows), F32)
     for c in range(chunks):
         cols = slice(c * chunk, (c + 1) * chunk)
-        arrive(errs.at[c, partner], forward + c)
+        arrive(errs.at[c, pl.ds(0, n - 1)], share + c)
         err = jnp.concatenate(
-            [errs[c, d // layers, d % layers].astype(F32) for d in range(n)], axis=0
+            [errs[c, d].astype(F32) for d in range(n)], axis=0
         ).astype(jnp.bfloat16)
         err_ref[:, cols] = err
         gd += lax.dot_general(
@@ -205,7 +190,7 @@
     for copy in copies:
         copy.start()
     err = err_ref[...]
-    step = 256
+    step = 128
     for i, r in enumerate(range(0, rows, step)):
         gw[r:r + step] = lax.dot_general(
             acts_ref[:, r:r + step], err, (((0,), (0,)), ((), ())), preferred_element_type=F32
@@ -245,16 +230,14 @@
             pltpu.VMEM((sources, 2, lanes), F32),
             pltpu.VMEM((n, 2, lanes), F32),
             pltpu.VMEM((everyone, rows // LANES, LANES), F32),
-            pltpu.VMEM((chunks, feats, layers, tokens, chunk), F32),
-            pltpu.VMEM((chunks, layers, tokens, chunk), F32),
-            pltpu.VMEM((chunks, layers, tokens, chunk), WIRE),
-            pltpu.VMEM((chunks, layers, tokens, chunk), WIRE),
-            pltpu.VMEM((chunks, feats, layers, tokens, chunk), jnp.bfloat16),
+            pltpu.VMEM((chunks, n, tokens, chunk), WIRE),
+            pltpu.VMEM((chunks, n, tokens, chunk), WIRE),
+            pltpu.VMEM((chunks, n, tokens, chunk), jnp.bfloat16),
             pltpu.VMEM((n, 1, lanes), F32),
             pltpu.VMEM((n, 1, lanes), F32),
             pltpu.SemaphoreType.DMA((3,)),
-            pltpu.SemaphoreType.DMA((2 + 4 * chunks,)),
-            pltpu.SemaphoreType.DMA((2 + 4 * chunks,)),
+            pltpu.SemaphoreType.DMA((2 + 2 * chunks,)),
+            pltpu.SemaphoreType.DMA((2 + 2 * chunks,)),
         ],
         compiler_params=pltpu.CompilerParams(
             collective_id=0, has_side_effects=True, vmem_limit_bytes=56 * 1024 * 1024
@@ -272,7 +255,7 @@
         scratch_shapes=[
             pltpu.VMEM((rows, width), jnp.bfloat16),
             pltpu.VMEM((tokens, sources, active), F32),
-            pltpu.SemaphoreType.DMA((2 + rows // 256,)),
+            pltpu.SemaphoreType.DMA((2 + rows // 128,)),
         ],
         compiler_params=pltpu.CompilerParams(vmem_limit_bytes=56 * 1024 * 1024),
     )(acts, err, recon, grad)

time: 33.4 us -> 32.5 us (0.973)
  Pallas kernels: 32.6 us -> 31.6 us
    pallas_call x1, Pallas kernels: 28.9 us -> 28.1 us  [per_device(): pl.pallas_call(exchange_kernel, out_shape=(jax.ShapeDtypeStruct((tokens,...]
where the time goes in v4:
time: 32.5 us; the launch traced here: 32.3 us
  Pallas kernels  31.6 us (97%)
  between operations  0.64 us (2%)
    pallas_call x1, Pallas kernels, per_device(): pl.pallas_call(exchange_kernel, out_shape=(jax.ShapeDtypeStruct((tokens,...  28.1 us
    pallas_call x1, Pallas kernels, per_device(): pl.pallas_call(finish_kernel, out_shape=(jax.ShapeDtypeStruct((tokens, wi...  3.53 us

profile of v4, /device:TPU:0, one launch (start us, length us, event | category | flops | bytes accessed | tf_op | source)
XLA Modules:
  0.0 32.3 jit_solution(6404283521984794064)
XLA Ops:
  0.6 28.1 %shard_map.76 = (f32[2,2304]{1,0:T(2,128)}, bf16[32,1024]{1,0:T(8,128)(2,1)}, bf16[32,2304]{1,0:T(8,128)(2,1)}, f32[1,1,128]{2,1,0:T(1,128)}) custom-call(s32[2,1,64]{2,1,0:T(1,128)} %idx_ref.1, bf16[1,2,64]{2,1,0:T(2,128)(2,1)} %bitcast.1, bf16[1024,2304]{1,0:T(8,128)(2,1)} %dec_hbm.1, f32[2304]{0:T(1024)} %bias_hbm.1, bf16[2,2304]{1,0:T(2,128)(2,1)} %target_hbm.1), custom_call_target="tpu_custom_call" | custom-call | tf_op jit(solution)/shard_map/pallas_call | solution.py:216
  28.7 3.5 %shard_map.77 = (f32[2,2304]{1,0:T(2,128)}, bf16[1024,2304]{1,0:T(8,128)(2,1)}, f32[2,1,64]{2,1,0:T(1,128)}) custom-call(bf16[32,1024]{1,0:T(8,128)(2,1)} %get-tuple-element.7.acts_ref, bf16[32,2304]{1,0:T(8,128)(2,1)} %get-tuple-element.8.err_ref, f32[2,2304]{1,0:T(2,128)} %get-tuple-element.9.recon_ref, f32[1,1,128]{2,1,0:T(1,128)} %get-tuple-element.10.grad_ref), custom_call_target="tpu_custom_call" | custom-call | tf_op jit(solution)/shard_map/pallas_call | solution.py:246

commit v5 on v4

--- a/solution.py
+++ b/solution.py
@@ -103,7 +103,7 @@
             a, onehot, (((1,), (1,)), ((), ())), preferred_element_type=F32)
         wide[pl.ds(d * tokens, tokens)] = spread.reshape(tokens, blocks, LANES)
         return carry
-    lax.fori_loop(0, n, build, 0, unroll=8)
+    lax.fori_loop(0, n, build, 0, unroll=16)
     acts = jnp.concatenate(
         [wide[:, h, :].astype(jnp.bfloat16) for h in range(blocks)], axis=1)
     acts_ref[...] = acts
@@ -155,7 +155,7 @@
         taken = taken[:rest_of] + taken[rest_of:2 * rest_of] + taken[2 * rest_of:]
         gout[d] = jnp.sum(jnp.where(mine, taken, 0.0), axis=0, keepdims=True)
         return carry
-    lax.fori_loop(0, n, pick, 0, unroll=8)
+    lax.fori_loop(0, n, pick, 0, unroll=16)
     others(lambda t: push(gout.at[t], gin.at[me], back, place(t)))
     gin[me] = gout[me]
     arrive(gin.at[pl.ds(0, n - 1)], back)

time: 32.5 us -> 32.1 us (0.988)
    pallas_call x1, Pallas kernels: 28.1 us -> 27.7 us  [per_device(): pl.pallas_call(exchange_kernel, out_shape=(jax.ShapeDtypeStruct((tokens,...]
where the time goes in v5:
time: 32.1 us; the launch traced here: 31.9 us
  Pallas kernels  31.3 us (98%)
  between operations  0.64 us (2%)
    pallas_call x1, Pallas kernels, per_device(): pl.pallas_call(exchange_kernel, out_shape=(jax.ShapeDtypeStruct((tokens,...  27.7 us
    pallas_call x1, Pallas kernels, per_device(): pl.pallas_call(finish_kernel, out_shape=(jax.ShapeDtypeStruct((tokens, wi...  3.53 us

profile of v5, /device:TPU:0, one launch (start us, length us, event | category | flops | bytes accessed | tf_op | source)
XLA Modules:
  0.0 31.9 jit_solution(6156846504054515903)
XLA Ops:
  0.6 27.7 %shard_map.76 = (f32[2,2304]{1,0:T(2,128)}, bf16[32,1024]{1,0:T(8,128)(2,1)}, bf16[32,2304]{1,0:T(8,128)(2,1)}, f32[1,1,128]{2,1,0:T(1,128)}) custom-call(s32[2,1,64]{2,1,0:T(1,128)} %idx_ref.1, bf16[1,2,64]{2,1,0:T(2,128)(2,1)} %bitcast.1, bf16[1024,2304]{1,0:T(8,128)(2,1)} %dec_hbm.1, f32[2304]{0:T(1024)} %bias_hbm.1, bf16[2,2304]{1,0:T(2,128)(2,1)} %target_hbm.1), custom_call_target="tpu_custom_call" | custom-call | tf_op jit(solution)/shard_map/pallas_call | solution.py:216
  28.4 3.5 %shard_map.77 = (f32[2,2304]{1,0:T(2,128)}, bf16[1024,2304]{1,0:T(8,128)(2,1)}, f32[2,1,64]{2,1,0:T(1,128)}) custom-call(bf16[32,1024]{1,0:T(8,128)(2,1)} %get-tuple-element.7.acts_ref, bf16[32,2304]{1,0:T(8,128)(2,1)} %get-tuple-element.8.err_ref, f32[2,2304]{1,0:T(2,128)} %get-tuple-element.9.recon_ref, f32[1,1,128]{2,1,0:T(1,128)} %get-tuple-element.10.grad_ref), custom_call_target="tpu_custom_call" | custom-call | tf_op jit(solution)/shard_map/pallas_call | solution.py:246
